TPU v7x, 512 devices: a whole 4x8x8 slice. The times are simulated.
512 devices in a mesh: region: 16 (over z, core), grp: 32 (over x, y).
Axes of the slice: x: 4, y: 8, z: 8, core: 2. Of those that a mesh axis runs over, the one named last changes fastest.
Arguments:
- ensemble: bfloat16 [256, 1024, 512], P('region', 'grp'), may hold values from -6 to 6
- obs_value: bfloat16 [1024, 512], P('grp'), may hold values from -8 to 8
- obs_prec: bfloat16 [1024, 512], P('grp'), may hold values from 0.25 to 4
- obs_index: int32 [32, 16, 256], P('grp', 'region'), may hold values from 0 to 4095, as said below
- obs_count: int32 [32, 16], P('grp', 'region'), may hold values from 0 to 256
Outputs:
- analysis: bfloat16 [256, 1024, 512], P('region', 'grp')
Inputs may be any that keep to these rules, and one draw needn't show every extreme that they name: `obs_index`: the first obs_count entries of a tile name distinct cells of its window, numbered row by row over 64 columns; the later entries are other window cells.
All inputs are finite; a program needn't handle non-finite values.
Results may differ from a plain program's by a relative error of at most 0.0058.
Values may be sent and summed in bfloat16 or wider, within the bound.
A program may use at most 64 MiB of HBM per device.

v0:
```python
import math

import jax
import jax.numpy as jnp
from jax import lax
from jax.sharding import PartitionSpec as P

TILE = 32
ITERS = 5


def with_halo(cells, sides, width):
    for axis, dim in sides:
        count = lax.axis_size(axis)
        ends = count - 1
        head = lax.slice_in_dim(cells, 0, width, axis=dim)
        tail = lax.slice_in_dim(cells, cells.shape[dim] - width, cells.shape[dim], axis=dim)
        cells = jnp.concatenate(
            [
                lax.ppermute(tail, axis, [(i, (i + 1) % count) for i in range(ends)]),
                cells,
                lax.ppermute(head, axis, [((i + 1) % count, i) for i in range(ends)]),
            ],
            axis=dim,
        )
    return cells


def inflation_coefficient(slot_cells, tile_cells):
    window = 2 * tile_cells
    centre = tile_cells - 0.5
    offset_y = (slot_cells // window).astype(jnp.float32) - centre
    offset_x = (slot_cells % window).astype(jnp.float32) - centre
    length = 0.375 * tile_cells
    return jnp.exp(-(offset_y * offset_y + offset_x * offset_x) / (2.0 * length * length))


def shards(ensemble, obs_value, obs_prec, obs_index, obs_count):
    regions = lax.axis_size("region")
    region_id = lax.axis_index("region")
    member_block, band_rows, column_total_grid = ensemble.shape
    tile_breadth = column_total_grid // regions
    border = TILE // 2
    window = 2 * TILE
    tiles_y = band_rows // TILE
    tiles_x = tile_breadth // TILE
    count_tiles = tiles_y * tiles_x
    slot_total = obs_index.shape[2]
    slot_cells = obs_index.reshape(count_tiles, slot_total)
    counts = obs_count.reshape(count_tiles)
    planes = jnp.stack([obs_value, obs_prec], 0)
    blocks = ensemble.reshape(member_block, band_rows, regions, tile_breadth)
    plane_blocks = planes.reshape(2, band_rows, regions, tile_breadth)
    arrived = lax.all_to_all(blocks, "region", split_axis=2, concat_axis=0, tiled=True)
    local_planes = lax.dynamic_index_in_dim(plane_blocks, region_id, 2, keepdims=False)
    joined = jnp.concatenate([arrived[:, :, 0, :], local_planes], 0)
    padded_layer_with_margin = with_halo(joined, (("region", 2), ("grp", 1)), border)
    sample_states = padded_layer_with_margin.shape[0] - 2
    prior_state_estimate = padded_layer_with_margin[:sample_states]
    sample_average_state = jnp.sum(prior_state_estimate, 0, dtype=jnp.float32) / sample_states
    sample_anomaly_vector = (
        prior_state_estimate.astype(jnp.float32) - sample_average_state
    ).astype(jnp.bfloat16)
    ext_rows = padded_layer_with_margin.shape[1]
    ext_cols = padded_layer_with_margin.shape[2]
    tile_ids = jnp.arange(count_tiles, dtype=jnp.int32)
    anchor = tile_ids // tiles_x * TILE * ext_cols + tile_ids % tiles_x * TILE
    located = anchor[:, None] + slot_cells // window * ext_cols + slot_cells % window
    obs_pert = jnp.transpose(
        jnp.take(
            sample_anomaly_vector.reshape(sample_states, ext_rows * ext_cols), located, axis=1
        ),
        (0, 1, 2),
    )
    innovation = jnp.take(
        padded_layer_with_margin[sample_states].reshape(ext_rows * ext_cols), located
    ).astype(jnp.float32) - jnp.take(sample_average_state.reshape(ext_rows * ext_cols), located)
    precision_at = jnp.take(
        padded_layer_with_margin[sample_states + 1].reshape(ext_rows * ext_cols), located
    ).astype(jnp.float32)
    interior = sample_anomaly_vector[:, border : border + band_rows, border : border + tile_breadth]
    interior_average = sample_average_state[
        border : border + band_rows, border : border + tile_breadth
    ]
    slot_ids = jnp.arange(slot_total, dtype=jnp.int32)
    live_slot = slot_ids[None, :] < counts[:, None]
    weight = jnp.where(
        live_slot, precision_at * inflation_coefficient(slot_cells, TILE), jnp.float32(0.0)
    )
    scaled_product = (obs_pert.astype(jnp.float32) * weight[None]).astype(jnp.bfloat16)
    gram_matrix = jnp.einsum(
        "inp,knp->nik", scaled_product, obs_pert, preferred_element_type=jnp.float32
    )
    highest = lax.Precision.HIGHEST
    identity = jnp.eye(sample_states, dtype=jnp.float32)
    system = (sample_states - 1.0) * identity + gram_matrix
    frobenius = jnp.sqrt(jnp.sum(system * system, axis=(1, 2)))
    matrix_square_root = system / frobenius[:, None, None]
    inverse_root = jnp.broadcast_to(identity, system.shape)
    for number in range(ITERS):
        weight_factor_matrix = 1.5 * identity - 0.5 * jnp.einsum(
            "nij,njk->nik", inverse_root, matrix_square_root, precision=highest
        )
        matrix_square_root = jnp.einsum(
            "nij,njk->nik", matrix_square_root, weight_factor_matrix, precision=highest
        )
        inverse_root = jnp.einsum(
            "nij,njk->nik", weight_factor_matrix, inverse_root, precision=highest
        )
    covariance = (
        jnp.einsum("nij,njk->nik", inverse_root, inverse_root, precision=highest)
        / frobenius[:, None, None]
    )
    projected = jnp.einsum(
        "np,knp->nk", innovation * weight, obs_pert.astype(jnp.float32), precision=highest
    )
    mean_weight = jnp.einsum("nik,nk->ni", covariance, projected, precision=highest)
    spread = math.sqrt(sample_states - 1.0) / jnp.sqrt(frobenius)
    weights = (spread[:, None, None] * inverse_root + mean_weight[:, :, None]).astype(jnp.bfloat16)
    interior = interior.reshape(sample_states, tiles_y, TILE, tiles_x, TILE)
    interior_average = interior_average.reshape(tiles_y, TILE, tiles_x, TILE)
    update = jnp.einsum(
        "iyaxb,yxik->kyaxb",
        interior,
        weights.reshape(tiles_y, tiles_x, sample_states, sample_states),
        preferred_element_type=jnp.float32,
    )
    analysis = (
        (update + interior_average)
        .astype(jnp.bfloat16)
        .reshape(sample_states, band_rows, tile_breadth)
    )
    returned = lax.all_to_all(
        analysis.reshape(regions, member_block, band_rows, tile_breadth),
        "region",
        split_axis=0,
        concat_axis=3,
        tiled=True,
    )
    return returned.reshape(member_block, band_rows, column_total_grid)


def solution(mesh):
    placed = (
        P("region", "grp", None),
        P("grp", None),
        P("grp", None),
        P("grp", "region", None),
        P("grp", "region"),
    )
    return jax.shard_map(
        shards, mesh=mesh, in_specs=placed, out_specs=P("region", "grp", None), check_vma=False
    )
```

profile of v0, /device:TPU:1, one launch (start us, length us, event | category | flops | bytes accessed | tf_op | source)
XLA Modules:
  0.0 130.7 jit_solution(651790646585770728)
XLA Ops:
  0.0 3.6 %reshape.797 = bf16[16,32,16,32]{3,2,1,0:T(8,128)(2,1)} reshape(bf16[16,32,512]{2,1,0:T(8,128)(2,1)} %param.7) | data formatting | bytes 1048576 | tf_op jit(solution)/shard_map/reshape | solution.py:52
  3.6 2.1 %copy.27 = bf16[16,32,16,32]{3,1,0,2:T(8,128)(2,1)S(1)} copy(bf16[16,32,16,32]{3,2,1,0:T(8,128)(2,1)} %reshape.797) | data formatting | bytes 1048576 | tf_op jit(solution)/shard_map/reshape | solution.py:52
  5.7 2.7 %reshape.855 = bf16[16,2,8192]{2,1,0:T(2,128)(2,1)} reshape(bf16[16,16,32,32]{3,2,1,0:T(8,128)(2,1)S(1)} %bitcast.122) | data formatting | bytes 1048576
  8.4 11.8 %all-to-all-start = ((bf16[16,2,8192]{2,1,0:T(2,128)(2,1)}), bf16[16,2,8192]{2,1,0:T(2,128)(2,1)S(1)}, u32[]{:S(2)}, u32[]{:S(2)}) async-start(bf16[16,2,8192]{2,1,0:T(2,128)(2,1)} %reshape.855), calls=%async_computation | async-start | bytes 1048576 | tf_op jit(solution)/shard_map/all_to_all | solution.py:54
  21.5 16.0 %all-to-all-done = bf16[16,2,8192]{2,1,0:T(2,128)(2,1)S(1)} async-done(((bf16[16,2,8192]{2,1,0:T(2,128)(2,1)}), bf16[16,2,8192]{2,1,0:T(2,128)(2,1)S(1)}, u32[]{:S(2)}, u32[]{:S(2)}) %all-to-all-start) | async-done | bytes 524320 | tf_op jit(solution)/shard_map/all_to_all | solution.py:54
  37.5 1.0 reshape.856
  38.5 1.7 %copy.23 = bf16[256,32,32]{0,2,1:T(8,128)(2,1)S(1)} copy(bf16[256,32,32]{2,1,0:T(8,128)(2,1)S(1)} %bitcast.120) | data formatting | bytes 1048576 | tf_op jit(solution)/shard_map/squeeze | solution.py:56
  40.3 1.9 %collective-permute-start = (bf16[258,32,16]{0,2,1:T(8,128)(2,1)S(1)}, bf16[258,32,16]{0,2,1:T(8,128)(2,1)S(1)}, u32[]{:S(2)}, u32[]{:S(2)}) collective-permute-start(bf16[258,32,16]{0,2,1:T(8,128)(2,1)S(1)} %get-tuple-element.13), channel_id=1, source_target_pairs={{0,32},{32,64},{64,96},{96,128},{128,160},{160,192},{192,224},{224... | collective-permute-start | bytes 792584 | tf_op jit(solution)/shard_map/ppermute | solution.py:20
  42.3 2.4 %collective-permute-start.1 = (bf16[258,32,16]{0,2,1:T(8,128)(2,1)S(1)}, bf16[258,32,16]{0,2,1:T(8,128)(2,1)S(1)}, u32[]{:S(2)}, u32[]{:S(2)}) collective-permute-start(bf16[258,32,16]{0,2,1:T(8,128)(2,1)S(1)} %get-tuple-element.14), channel_id=1, source_target_pairs={{32,0},{64,32},{96,64},{128,96},{160,128},{192,160},{224,192},{256... | collective-permute-start | bytes 792584 | tf_op jit(solution)/shard_map/ppermute | solution.py:22
  44.7 2.2 %collective-permute-done = bf16[258,32,16]{0,2,1:T(8,128)(2,1)S(1)} collective-permute-done((bf16[258,32,16]{0,2,1:T(8,128)(2,1)S(1)}, bf16[258,32,16]{0,2,1:T(8,128)(2,1)S(1)}, u32[]{:S(2)}, u32[]{:S(2)}) %collective-permute-start) | collective-permute-done | bytes 264224 | tf_op jit(solution)/shard_map/ppermute | solution.py:20
  47.0 4.4 %collective-permute-done.1 = bf16[258,32,16]{0,2,1:T(8,128)(2,1)S(1)} collective-permute-done((bf16[258,32,16]{0,2,1:T(8,128)(2,1)S(1)}, bf16[258,32,16]{0,2,1:T(8,128)(2,1)S(1)}, u32[]{:S(2)}, u32[]{:S(2)}) %collective-permute-start.1) | collective-permute-done | bytes 264224 | tf_op jit(solution)/shard_map/ppermute | solution.py:22
  51.7 3.2 %collective-permute-start.2 = (bf16[258,16,64]{0,2,1:T(8,128)(2,1)S(1)}, bf16[258,16,64]{0,2,1:T(8,128)(2,1)S(1)}, u32[]{:S(2)}, u32[]{:S(2)}) collective-permute-start(bf16[258,16,64]{0,2,1:T(8,128)(2,1)S(1)} %get-tuple-element.11), channel_id=1, source_target_pairs={{0,1},{1,2},{2,3},{3,4},{4,5},{5,6},{6,7},{7,8},{8,9},{9,10},{10,1... | collective-permute-start | bytes 1585160 | tf_op jit(solution)/shard_map/ppermute | solution.py:20
  55.0 1.5 %collective-permute-start.3 = (bf16[258,16,64]{0,2,1:T(8,128)(2,1)S(1)}, bf16[258,16,64]{0,2,1:T(8,128)(2,1)S(1)}, u32[]{:S(2)}, u32[]{:S(2)}) collective-permute-start(bf16[258,16,64]{0,2,1:T(8,128)(2,1)S(1)} %get-tuple-element.12), channel_id=1, source_target_pairs={{1,0},{2,1},{3,2},{4,3},{5,4},{6,5},{7,6},{8,7},{9,8},{10,9},{11,1... | collective-permute-start | bytes 1585160 | tf_op jit(solution)/shard_map/ppermute | solution.py:22
  56.5 11.3 %collective-permute-done.2 = bf16[258,16,64]{0,2,1:T(8,128)(2,1)S(1)} collective-permute-done((bf16[258,16,64]{0,2,1:T(8,128)(2,1)S(1)}, bf16[258,16,64]{0,2,1:T(8,128)(2,1)S(1)}, u32[]{:S(2)}, u32[]{:S(2)}) %collective-permute-start.2) | collective-permute-done | bytes 528416 | tf_op jit(solution)/shard_map/ppermute | solution.py:20
  67.8 4.1 %collective-permute-done.3 = bf16[258,16,64]{0,2,1:T(8,128)(2,1)S(1)} collective-permute-done((bf16[258,16,64]{0,2,1:T(8,128)(2,1)S(1)}, bf16[258,16,64]{0,2,1:T(8,128)(2,1)S(1)}, u32[]{:S(2)}, u32[]{:S(2)}) %collective-permute-start.3) | collective-permute-done | bytes 528416 | tf_op jit(solution)/shard_map/ppermute | solution.py:22
  71.9 1.3 pad_maximum_fusion
  73.2 0.6 convert_reduce_fusion
  73.8 1.5 %slice_reduce_fusion = (bf16[64,64]{1,0:T(8,128)(2,1)S(1)}, bf16[64,64]{1,0:T(8,128)(2,1)S(1)}) fusion(bf16[258,64,64]{0,2,1:T(8,128)(2,1)S(1)} %pad_maximum_fusion), kind=kLoop, calls=%fused_computation.22 | loop fusion | bytes 32768 | tf_op jit(solution)/shard_map/slice | solution.py:76
  75.3 0.7 fusion
  76.2 1.2 gather_fusion
  77.4 1.9 %gather_fusion.2 = bf16[256]{0:T(256)(128)(2,1)S(1)} fusion(bf16[4096]{0:T(1024)(128)(2,1)S(1)} %reshape_squeeze.6, s32[1024]{0:T(1024)S(1)} %pad_clamp_fusion), kind=kCustom, calls=%fused_computation.clone | custom fusion | bytes 2048 | tf_op jit(solution)/shard_map/jit(_take)/gather | solution.py:78
  79.3 1.0 multiply_reduce_fusion
  81.3 0.4 fusion.16
  85.7 1.9 %gather_fusion.3 = bf16[256]{0:T(256)(128)(2,1)S(1)} fusion(bf16[4096]{0:T(1024)(128)(2,1)S(1)} %reshape_squeeze.7, s32[1024]{0:T(1024)S(1)} %pad_clamp_fusion), kind=kCustom, calls=%fused_computation.1.clone | custom fusion | bytes 2048 | tf_op jit(solution)/shard_map/jit(_take)/gather | solution.py:75
  87.7 1.7 %gather_fusion.1 = f32[256]{0:T(256)S(1)} fusion(f32[4096]{0:T(1024)S(1)} %div.87, s32[1024]{0:T(1024)S(1)} %pad_clamp_fusion.1), kind=kCustom, calls=%fused_computation.3 | custom fusion | bytes 3072 | tf_op jit(solution)/shard_map/jit(_take)/gather | solution.py:77
  91.1 0.4 fusion.10
  91.7 3.2 %copy.24 = bf16[256,32,32]{2,1,0:T(8,128)(2,1)S(1)} copy(bf16[256,32,32]{0,2,1:T(8,128)(2,1)S(1)} %add_convert_fusion) | data formatting | bytes 1048576 | tf_op jit(solution)/shard_map/convert_element_type | solution.py:130
  95.0 2.0 %reshape.857 = bf16[16,2,8192]{2,1,0:T(2,128)(2,1)S(1)} reshape(bf16[16,16,32,32]{3,2,1,0:T(8,128)(2,1)S(1)} %bitcast.121) | data formatting | bytes 1048576
  96.9 26.0 %all_to_all.30 = bf16[16,2,8192]{2,1,0:T(2,128)(2,1)S(1)} all-to-all(bf16[16,2,8192]{2,1,0:T(2,128)(2,1)S(1)} %reshape.857), channel_id=1, replica_groups=mesh['region'=16,'grp'=32] {'region'}, dimensions={0} | all-to-all | bytes 1048576 | tf_op jit(solution)/shard_map/all_to_all | solution.py:133
  122.9 1.0 reshape.858
  124.0 2.7 %copy.25 = bf16[1,16,32,16,32]{4,3,2,1,0:T(8,128)(2,1)} copy(bf16[1,16,32,16,32]{4,2,1,3,0:T(8,128)(2,1)S(1)} %bitcast.123) | data formatting | bytes 1048576 | tf_op jit(solution)/shard_map/all_to_all | solution.py:133
  126.7 4.1 %reshape.802 = bf16[16,32,512]{2,1,0:T(8,128)(2,1)} reshape(bf16[1,16,32,16,32]{4,3,2,1,0:T(8,128)(2,1)} %copy.25) | data formatting | bytes 1048576 | tf_op jit(solution)/shard_map/reshape | solution.py:140
  (43 shorter events, 7.4 us)
Async XLA Ops:
  3.6 16.6 %copy-start = (bf16[32,512]{1,0:T(8,128)(2,1)S(1)}, bf16[32,512]{1,0:T(8,128)(2,1)}, u32[]{:S(2)}) copy-start(bf16[32,512]{1,0:T(8,128)(2,1)} %param.9) | copy-start | bytes 98308
  3.6 16.8 %copy-start.1 = (bf16[32,512]{1,0:T(8,128)(2,1)S(1)}, bf16[32,512]{1,0:T(8,128)(2,1)}, u32[]{:S(2)}) copy-start(bf16[32,512]{1,0:T(8,128)(2,1)} %param.8) | copy-start | bytes 98308
  8.4 29.2 %all-to-all-start = ((bf16[16,2,8192]{2,1,0:T(2,128)(2,1)}), bf16[16,2,8192]{2,1,0:T(2,128)(2,1)S(1)}, u32[]{:S(2)}, u32[]{:S(2)}) async-start(bf16[16,2,8192]{2,1,0:T(2,128)(2,1)} %reshape.855), calls=%async_computation | async-start | bytes 1048576 | tf_op jit(solution)/shard_map/all_to_all | solution.py:54
  21.5 23.2 %copy-start.2 = (s32[1,1,256]{2,1,0:T(1,128)S(1)}, s32[1,1,256]{2,1,0:T(1,128)}, u32[]{:S(2)}) copy-start(s32[1,1,256]{2,1,0:T(1,128)} %param.10) | copy-start | bytes 3076
  40.3 6.6 %collective-permute-start = (bf16[258,32,16]{0,2,1:T(8,128)(2,1)S(1)}, bf16[258,32,16]{0,2,1:T(8,128)(2,1)S(1)}, u32[]{:S(2)}, u32[]{:S(2)}) collective-permute-start(bf16[258,32,16]{0,2,1:T(8,128)(2,1)S(1)} %get-tuple-element.13), channel_id=1, source_target_pairs={{0,32},{32,64},{64,96},{96,128},{128,160},{160,192},{192,224},{224... | collective-permute-start | bytes 792584 | tf_op jit(solution)/shard_map/ppermute | solution.py:20
  42.3 9.1 %collective-permute-start.1 = (bf16[258,32,16]{0,2,1:T(8,128)(2,1)S(1)}, bf16[258,32,16]{0,2,1:T(8,128)(2,1)S(1)}, u32[]{:S(2)}, u32[]{:S(2)}) collective-permute-start(bf16[258,32,16]{0,2,1:T(8,128)(2,1)S(1)} %get-tuple-element.14), channel_id=1, source_target_pairs={{32,0},{64,32},{96,64},{128,96},{160,128},{192,160},{224,192},{256... | collective-permute-start | bytes 792584 | tf_op jit(solution)/shard_map/ppermute | solution.py:22
  51.7 16.1 %collective-permute-start.2 = (bf16[258,16,64]{0,2,1:T(8,128)(2,1)S(1)}, bf16[258,16,64]{0,2,1:T(8,128)(2,1)S(1)}, u32[]{:S(2)}, u32[]{:S(2)}) collective-permute-start(bf16[258,16,64]{0,2,1:T(8,128)(2,1)S(1)} %get-tuple-element.11), channel_id=1, source_target_pairs={{0,1},{1,2},{2,3},{3,4},{4,5},{5,6},{6,7},{7,8},{8,9},{9,10},{10,1... | collective-permute-start | bytes 1585160 | tf_op jit(solution)/shard_map/ppermute | solution.py:20
  55.0 16.9 %collective-permute-start.3 = (bf16[258,16,64]{0,2,1:T(8,128)(2,1)S(1)}, bf16[258,16,64]{0,2,1:T(8,128)(2,1)S(1)}, u32[]{:S(2)}, u32[]{:S(2)}) collective-permute-start(bf16[258,16,64]{0,2,1:T(8,128)(2,1)S(1)} %get-tuple-element.12), channel_id=1, source_target_pairs={{1,0},{2,1},{3,2},{4,3},{5,4},{6,5},{7,6},{8,7},{9,8},{10,9},{11,1... | collective-permute-start | bytes 1585160 | tf_op jit(solution)/shard_map/ppermute | solution.py:22
where the time goes:
time: 133 us; the launch traced here: 131 us
  waiting for transfers between devices  38 us (29%)
  local copies, waits for them, and re-layouts  33.4 us (25%)
  blocking collectives  26 us (20%)
  starting transfers between devices  20.9 us (16%)
  matrix products  7.46 us (6%)
  other arithmetic  3.24 us (2%)
  between operations  1.79 us (1%)
    all_to_all x1, blocking collectives, shards(): lax.all_to_all(analysis.reshape(regions, member_block, band_rows, tile_br...  26 us
    all_to_all x1, waiting for transfers between devices, shards(): lax.all_to_all(blocks, 'region', split_axis=2, concat_axis=0, tiled=True)  16 us
    ppermute x2, waiting for transfers between devices, with_halo(): lax.ppermute(tail, axis, [(i, (i + 1) % count) for i in range(ends)])  13.5 us
    all_to_all x1, starting transfers between devices, shards(): lax.all_to_all(blocks, 'region', split_axis=2, concat_axis=0, tiled=True)  11.8 us
    ppermute x2, waiting for transfers between devices, with_halo(): lax.ppermute(head, axis, [((i + 1) % count, i) for i in range(ends)])  8.54 us
    unnamed x10, local copies, waits for them, and re-layouts  6.67 us
    reshape x2, local copies, waits for them, and re-layouts, shards(): blocks = ensemble.reshape(member_block, band_rows, regions, tile_breadth)  5.69 us
    ppermute x2, starting transfers between devices, with_halo(): lax.ppermute(tail, axis, [(i, (i + 1) % count) for i in range(ends)])  5.17 us
  transfers between devices with their start and end apart: 5, of which 5 were waited for; matrix products, arithmetic and copies ran while one was open for 1% of the time, Pallas kernels for 0%

commit v1 on v0

v1 whole, which is shorter than its diff:
```python
import functools
import math

import jax
import jax.numpy as jnp
from jax import lax
from jax.experimental import pallas as pl
from jax.experimental.pallas import tpu as pltpu
from jax.sharding import PartitionSpec as P

TILE = 32
ITERS = 5
LANES = 128
MESH = pl.DeviceIdType.MESH
F32 = jnp.float32
BF16 = jnp.bfloat16


def swap_blocks(parts):
    lane = lax.broadcasted_iota(jnp.int32, parts[0].shape, 1)
    low = lane < 64
    even = (lane // 32) % 2 == 0
    half = []
    for a, b in ((parts[0], parts[2]), (parts[1], parts[3])):
        half.append(
            (
                jnp.where(low, a, pltpu.roll(b, 64, 1)),
                jnp.where(low, pltpu.roll(a, 64, 1), b),
            )
        )
    result = []
    for which in range(2):
        a, b = half[0][which], half[1][which]
        result.append(jnp.where(even, a, pltpu.roll(b, 32, 1)))
        result.append(jnp.where(even, pltpu.roll(a, 96, 1), b))
    return result


def split(a):
    high = a.astype(BF16)
    return high, (a - high.astype(F32)).astype(BF16)


def product(a, b):
    return (
        jnp.dot(a[0], b[0], preferred_element_type=F32)
        + jnp.dot(a[0], b[1], preferred_element_type=F32)
        + jnp.dot(a[1], b[0], preferred_element_type=F32)
    )


def window_base(tile):
    return jnp.clip((tile * TILE + LANES - TILE // 2) // LANES - 1, 0, 2)


def column_select(cells, tile):
    base = window_base(tile)
    column = cells % (2 * TILE) + (tile * TILE - TILE // 2 - base * LANES)
    place = lax.broadcasted_iota(jnp.int32, (2 * LANES, cells.shape[1]), 0)
    return jnp.where(place == column, F32(1.0), F32(0.0)).astype(BF16)


def row_select(columns, rows, members):
    slots = columns.shape[1]
    parts = columns.reshape(members, 4, 8, slots)
    place = lax.broadcasted_iota(jnp.int32, (8, slots), 0)
    chosen = jnp.zeros((members, 8, slots), F32)
    for q in range(4):
        mask = jnp.broadcast_to((place + 8 * q == rows)[None], chosen.shape)
        chosen = jnp.where(mask, parts[:, q], chosen)
    return chosen.reshape(members * 8, slots)


def own_rows(cells):
    return cells // (2 * TILE) - TILE // 2


def halo_rows(cells, first, last):
    row = cells // (2 * TILE)
    above = jnp.where(first, -1, row)
    below = jnp.where(last, -1, row - TILE)
    return jnp.where(row < TILE // 2, above, jnp.where(row >= 3 * TILE // 2, below, -1))


def kernel(
    regions,
    bands,
    ens,
    value,
    precision,
    index,
    count,
    out,
    held,
    halo,
    planes,
    cells_all,
    shuffle,
    main_send,
    main_recv,
    selected,
    obs_send,
    obs_recv,
    back_send,
    back_recv,
    result,
    load_sem,
    halo_sems,
    plane_sems,
    cell_sems,
    main_sems,
    obs_sems,
    back_sems,
    out_sems,
):
    r = lax.axis_index("region")
    g = lax.axis_index("grp")
    up = lax.rem(g + bands - 1, bands)
    down = lax.rem(g + 1, bands)
    members = ens.shape[0]
    total = members * regions
    half = TILE // 2
    slots = index.shape[2]
    groups = regions // 4

    def peer(d):
        return lax.rem(r + d, regions)

    barrier = pltpu.get_barrier_semaphore()

    def greet(d, carry):
        pl.semaphore_signal(barrier, inc=1, device_id={"region": peer(d)}, device_id_type=MESH)
        return carry

    load = pltpu.make_async_copy(ens, held, load_sem)
    load.start()
    for band in (up, down):
        pl.semaphore_signal(barrier, inc=1, device_id={"grp": band}, device_id_type=MESH)
    lax.fori_loop(1, regions, greet, 0)
    cells_all[r] = index[0]
    load.wait()
    pl.semaphore_wait(barrier, regions + 1)

    base_lanes = pl.ds(pl.multiple_of(window_base(r) * LANES, LANES), 2 * LANES)

    def halo_copy(side):
        band = (down, up)[side]
        rows = (pl.ds(half, half), pl.ds(0, half))[side]
        place = pl.ds(side * half, half)
        pairs = [(held.at[:, rows, :], halo.at[:, place, :], halo_sems, side)]
        for n, plane in enumerate((value, precision)):
            pairs.append((plane.at[rows, base_lanes], planes.at[n, place, :], plane_sems, 2 * n + side))
        return [
            pltpu.make_async_remote_copy(
                src_ref=src,
                dst_ref=dst,
                send_sem=sems.at[0, at],
                recv_sem=sems.at[1, at],
                device_id={"grp": band},
                device_id_type=MESH,
            )
            for src, dst, sems, at in pairs
        ]

    def cell_copy(to, slot):
        return pltpu.make_async_remote_copy(
            src_ref=cells_all.at[r],
            dst_ref=cells_all.at[slot],
            send_sem=cell_sems.at[0, to],
            recv_sem=cell_sems.at[1, slot],
            device_id={"region": to},
            device_id_type=MESH,
        )

    def block_copy(send, recv, sems, to, slot):
        return pltpu.make_async_remote_copy(
            src_ref=send.at[to],
            dst_ref=recv.at[slot],
            send_sem=sems.at[0, to],
            recv_sem=sems.at[1, slot],
            device_id={"region": to},
            device_id_type=MESH,
        )

    def send_cells(d, carry):
        cell_copy(peer(d), r).start()
        return carry

    lax.fori_loop(1, regions, send_cells, 0)
    halo_copies = halo_copy(0) + halo_copy(1)
    for copy in halo_copies:
        copy.start()

    def pack_group(step, carry):
        group = lax.rem(r // 4 + step, groups)
        lanes = pl.ds(pl.multiple_of(group * LANES, LANES), LANES)

        def pack_member(m, inner):
            block = held[m, :, lanes].astype(F32)
            parts = swap_blocks([block[8 * q : 8 * q + 8] for q in range(4)])
            at = pl.ds(pl.multiple_of(m * 8, 8), 8)
            for t in range(4):
                shuffle[t, at, :] = parts[t]
            return inner

        lax.fori_loop(0, members, pack_member, 0)

        for t in range(4):
            tile = 4 * group + t
            for s in range(8):
                main_send[tile, :, s * LANES : (s + 1) * LANES] = shuffle[
                    t, pl.ds(s, members, stride=8), :
                ].astype(BF16)

            @pl.when(tile != r)
            def _():
                block_copy(main_send, main_recv, main_sems, tile, r).start()

            @pl.when(tile == r)
            def _():
                main_recv[r] = main_send[r]

        return carry

    lax.fori_loop(0, groups, pack_group, 0)

    gather_rows = lax.broadcasted_iota(jnp.int32, (members, members * 8), 0)
    gather_cols = lax.broadcasted_iota(jnp.int32, (members, members * 8), 1)
    fold = jnp.where(gather_cols // 8 == gather_rows, F32(1.0), F32(0.0)).astype(BF16)

    def choose(source, cells, rows, tile):
        lanes = pl.ds(pl.multiple_of(window_base(tile) * LANES, LANES), 2 * LANES)
        columns = jnp.dot(
            source[:, :, lanes].reshape(members * TILE, 2 * LANES),
            column_select(cells, tile),
            preferred_element_type=F32,
        )
        picked = row_select(columns, rows, members).astype(BF16)
        return jnp.dot(fold, picked, preferred_element_type=F32)

    def from_own(d, carry):
        tile = peer(d)

        @pl.when(tile != r)
        def _():
            cell_copy(tile, tile).wait_recv()

        cells = cells_all[tile]
        selected[tile] = choose(held, cells, own_rows(cells), tile)
        return carry

    lax.fori_loop(0, regions, from_own, 0)

    for copy in halo_copies:
        copy.wait_recv()

    def from_halo(d, carry):
        tile = peer(d)
        cells = cells_all[tile]
        rows = halo_rows(cells, g == 0, g == bands - 1)
        obs_send[tile] = (selected[tile] + choose(halo, cells, rows, tile)).astype(BF16)
        block_copy(obs_send, obs_recv, obs_sems, tile, r).start()
        return carry

    lax.fori_loop(1, regions, from_halo, 0)
    cells = cells_all[r]
    rows_own = own_rows(cells)
    rows_halo = halo_rows(cells, g == 0, g == bands - 1)
    obs_recv[r] = (selected[r] + choose(halo, cells, rows_halo, r)).astype(BF16)

    fields = jnp.concatenate(
        [value[:, base_lanes], planes[0], precision[:, base_lanes], planes[1]], axis=0
    )
    columns = jnp.dot(fields, column_select(cells, r), preferred_element_type=F32)
    place = lax.broadcasted_iota(jnp.int32, (TILE, slots), 0)
    at_own = place == rows_own
    at_halo = place == rows_halo

    def field(n):
        own = jnp.where(at_own, columns[2 * n * TILE : (2 * n + 1) * TILE], F32(0.0))
        beside = jnp.where(at_halo, columns[(2 * n + 1) * TILE : (2 * n + 2) * TILE], F32(0.0))
        return jnp.sum(own + beside, axis=0, keepdims=True)

    values_at = field(0)
    precision_at = field(1)
    offset_y = (cells // (2 * TILE)).astype(F32) - (TILE - 0.5)
    offset_x = (cells % (2 * TILE)).astype(F32) - (TILE - 0.5)
    length = 0.375 * TILE
    inflation = jnp.exp(-(offset_y * offset_y + offset_x * offset_x) / (2.0 * length * length))
    live = lax.broadcasted_iota(jnp.int32, (1, slots), 1) < count[0, 0]
    weight = jnp.where(live, precision_at * inflation, F32(0.0))

    def wait_block(recv, sems):
        def body(d, carry):
            src = peer(d)
            block_copy(recv, recv, sems, src, src).wait_recv()
            return carry

        lax.fori_loop(1, regions, body, 0)

    wait_block(obs_recv, obs_sems)

    raw = obs_recv[...].reshape(total, slots).astype(F32)
    average = jnp.sum(raw, axis=0, keepdims=True) * (1.0 / total)
    pert = (raw - average).astype(BF16)
    scaled = weight * (values_at - average)
    weighted = (pert.astype(F32) * weight).astype(BF16)
    across = (((1,), (1,)), ((), ()))
    diagonal = lax.broadcasted_iota(jnp.int32, (total, total), 0) == lax.broadcasted_iota(
        jnp.int32, (total, total), 1
    )

    def plus_identity(scale, a):
        return a + jnp.where(diagonal, F32(scale), F32(0.0))

    system = plus_identity(
        total - 1.0, lax.dot_general(pert, weighted, across, preferred_element_type=F32)
    )
    squares = jnp.sum(system * system, axis=0, keepdims=True)
    frobenius = jnp.sqrt(jnp.sum(squares, axis=1, keepdims=True))
    inverse_frobenius = 1.0 / frobenius

    scaled_high = scaled.astype(BF16)
    rest = scaled - scaled_high.astype(F32)
    scaled_mid = rest.astype(BF16)
    scaled_low = (rest - scaled_mid.astype(F32)).astype(BF16)

    def stack(*rows):
        n = rows[0].shape[1]
        place = lax.broadcasted_iota(jnp.int32, (16, n), 0)
        whole = jnp.zeros((16, n), F32)
        for at, row in enumerate(rows):
            whole = jnp.where(place == at, row.astype(F32), whole)
        return whole.astype(BF16)

    projected = jnp.sum(
        lax.dot_general(
            stack(scaled_high, scaled_mid, scaled_low), pert, across, preferred_element_type=F32
        ),
        axis=0,
        keepdims=True,
    )

    start = system * inverse_frobenius
    root = split(start)
    inverse_root = plus_identity(1.5, -0.5 * start)
    factor = split(inverse_root)
    inverse_pair = factor
    root = split(product(root, factor))
    for number in range(1, ITERS):
        factor = split(plus_identity(1.5, -0.5 * product(root, inverse_pair)))
        if number < ITERS - 1:
            root = split(product(factor, root))
        inverse_root = product(inverse_pair, factor)
        inverse_pair = split(inverse_root)

    def row_product(row):
        pair = stack(*split(row))
        first = jnp.dot(pair, inverse_pair[0], preferred_element_type=F32)
        second = jnp.dot(pair, inverse_pair[1], preferred_element_type=F32)
        return first[0:1] + first[1:2] + second[0:1]

    mean_weight = row_product(row_product(projected)) * inverse_frobenius
    spread = math.sqrt(total - 1.0) / jnp.sqrt(frobenius)
    weights = (spread * inverse_root + mean_weight).astype(BF16)

    wait_block(main_recv, main_sems)
    cell_total = main_recv.shape[2]
    step = 2 * LANES
    for n in range(cell_total // step):
        at = slice(n * step, (n + 1) * step)
        prior = main_recv[:, :, at].reshape(total, step).astype(F32)
        mean = jnp.sum(prior, axis=0, keepdims=True) * (1.0 / total)
        update = jnp.dot(weights, (prior - mean).astype(BF16), preferred_element_type=F32)
        back_send[:, :, at] = (update + mean).astype(BF16).reshape(regions, members, step)

    def send_back(d, carry):
        block_copy(back_send, back_recv, back_sems, peer(d), r).start()
        return carry

    lax.fori_loop(1, regions, send_back, 0)
    back_recv[r] = back_send[r]

    def out_copy(group):
        lanes = pl.ds(pl.multiple_of(group * LANES, LANES), LANES)
        return pltpu.make_async_copy(result.at[:, :, lanes], out.at[:, :, lanes], out_sems.at[group])

    def unpack_group(step, carry):
        group = lax.rem(r // 4 + step, groups)
        lanes = pl.ds(pl.multiple_of(group * LANES, LANES), LANES)
        for t in range(4):
            tile = 4 * group + t

            @pl.when(tile != r)
            def _():
                block_copy(back_recv, back_recv, back_sems, tile, tile).wait_recv()

            for s in range(8):
                shuffle[t, pl.ds(s, members, stride=8), :] = back_recv[
                    tile, :, s * LANES : (s + 1) * LANES
                ].astype(F32)

        def unpack_member(m, inner):
            at = pl.ds(pl.multiple_of(m * 8, 8), 8)
            parts = swap_blocks([shuffle[t, at, :] for t in range(4)])
            result[m, :, lanes] = jnp.concatenate(parts, axis=0).astype(BF16)
            return inner

        lax.fori_loop(0, members, unpack_member, 0)
        out_copy(group).start()
        return carry

    lax.fori_loop(0, groups, unpack_group, 0)

    def finish_sends(d, carry):
        to = peer(d)
        cell_copy(to, r).wait_send()
        block_copy(main_send, main_recv, main_sems, to, r).wait_send()
        block_copy(obs_send, obs_recv, obs_sems, to, r).wait_send()
        block_copy(back_send, back_recv, back_sems, to, r).wait_send()
        return carry

    lax.fori_loop(1, regions, finish_sends, 0)
    for copy in halo_copies:
        copy.wait_send()

    def finish_out(group, carry):
        out_copy(group).wait()
        return carry

    lax.fori_loop(0, groups, finish_out, 0)


def solution(mesh):
    regions = mesh.shape["region"]
    bands = mesh.shape["grp"]

    def shards(ensemble, obs_value, obs_prec, obs_index, obs_count):
        members, rows, columns = ensemble.shape
        slots = obs_index.shape[2]
        cells = rows * TILE
        total = members * regions
        vmem = pl.BlockSpec(memory_space=pltpu.VMEM)
        hbm = pl.BlockSpec(memory_space=pl.ANY)
        return pl.pallas_call(
            functools.partial(kernel, regions, bands),
            out_shape=jax.ShapeDtypeStruct(ensemble.shape, BF16),
            in_specs=[hbm, vmem, vmem, vmem, pl.BlockSpec(memory_space=pltpu.SMEM)],
            out_specs=hbm,
            scratch_shapes=[
                pltpu.VMEM((members, rows, columns), BF16),
                pltpu.VMEM((members, rows, columns), BF16),
                pltpu.VMEM((2, rows, 2 * LANES), BF16),
                pltpu.VMEM((regions, 1, slots), jnp.int32),
                pltpu.VMEM((4, members * 8, LANES), F32),
                pltpu.VMEM((regions, members, cells), BF16),
                pltpu.VMEM((regions, members, cells), BF16),
                pltpu.VMEM((regions, members, slots), F32),
                pltpu.VMEM((regions, members, slots), BF16),
                pltpu.VMEM((regions, members, slots), BF16),
                pltpu.VMEM((regions, members, cells), BF16),
                pltpu.VMEM((regions, members, cells), BF16),
                pltpu.VMEM((members, rows, columns), BF16),
                pltpu.SemaphoreType.DMA,
                pltpu.SemaphoreType.DMA((2, 2)),
                pltpu.SemaphoreType.DMA((2, 4)),
                pltpu.SemaphoreType.DMA((2, regions)),
                pltpu.SemaphoreType.DMA((2, regions)),
                pltpu.SemaphoreType.DMA((2, regions)),
                pltpu.SemaphoreType.DMA((2, regions)),
                pltpu.SemaphoreType.DMA((regions // 4,)),
            ],
            compiler_params=pltpu.CompilerParams(
                collective_id=0, has_side_effects=True, vmem_limit_bytes=32 * 1024 * 1024
            ),
        )(ensemble, obs_value, obs_prec, obs_index, obs_count)

    placed = (
        P("region", "grp", None),
        P("grp", None),
        P("grp", None),
        P("grp", "region", None),
        P("grp", "region"),
    )
    return jax.shard_map(
        shards, mesh=mesh, in_specs=placed, out_specs=P("region", "grp", None), check_vma=False
    )
```

time: 133 us -> 71.4 us (0.54); the launches traced: 131 us -> 71 us
  Pallas kernels: 0 us -> 67 us
  waiting for transfers between devices: 38 us -> 0 us
  local copies, waits for them, and re-layouts: 33.4 us -> 3.36 us
  blocking collectives: 26 us -> 0 us
  starting transfers between devices: 20.9 us -> 0 us
  matrix products: 7.46 us -> 0 us
  other arithmetic: 3.24 us -> 0 us
    pallas_call x0 -> x1, Pallas kernels: none -> 67 us  [shards(): pl.pallas_call(functools.partial(kernel, regions, bands), out_shape=jax.S...]
    all_to_all x1 -> x0, blocking collectives: 26 us -> none  [shards(): lax.all_to_all(analysis.reshape(regions, member_block, band_rows, tile_br...]
    ppermute x4 -> x0, waiting for transfers between devices: 22 us -> none  [the longest x2 13.5 us: with_halo(): lax.ppermute(tail, axis, [(i, (i + 1) % count) for i in range(ends)])]
    all_to_all x1 -> x0, waiting for transfers between devices: 16 us -> none  [shards(): lax.all_to_all(blocks, 'region', split_axis=2, concat_axis=0, tiled=True)]
    all_to_all x1 -> x0, starting transfers between devices: 11.8 us -> none  [shards(): lax.all_to_all(blocks, 'region', split_axis=2, concat_axis=0, tiled=True)]
    reshape x3 -> x0, local copies, waits for them, and re-layouts: 9.78 us -> none  [the longest x2 5.69 us: shards(): blocks = ensemble.reshape(member_block, band_rows, regions, tile_breadth)]
    ppermute x4 -> x0, starting transfers between devices: 9.07 us -> none  [the longest x2 5.17 us: with_halo(): lax.ppermute(tail, axis, [(i, (i + 1) % count) for i in range(ends)])]
    dot_general x18 -> x0, matrix products: 7.04 us -> none  [the longest x5 1.84 us: shards(): jnp.einsum('nij,njk->nik', inverse_root, matrix_square_root, precision=hi...]
  transfers between devices with their start and end apart: 5 -> 0, of which waited for: 5 -> 0; matrix products, arithmetic and copies ran while one was open for 1% -> 0% of each run, Pallas kernels for 0% -> 0%
where the time goes in v1:
time: 71.4 us; the launch traced here: 71 us
  Pallas kernels  67 us (94%)
  local copies, waits for them, and re-layouts  3.36 us (5%)
    pallas_call x1, Pallas kernels, shards(): pl.pallas_call(functools.partial(kernel, regions, bands), out_shape=jax.S...  67 us
    unnamed x9, local copies, waits for them, and re-layouts  3.36 us

profile of v1, /device:TPU:1, one launch (start us, length us, event | category | flops | bytes accessed | tf_op | source)
XLA Modules:
  0.0 71.0 jit_solution(12631187159030894155)
XLA Ops:
  0.0 0.0 copy-start.3
  0.7 0.0 copy-done.3
  0.7 0.0 copy-start
  0.7 1.0 %copy-done = bf16[16,32,512]{2,1,0:T(8,128)(2,1)S(1)} copy-done((bf16[16,32,512]{2,1,0:T(8,128)(2,1)S(1)}, bf16[16,32,512]{2,1,0:T(8,128)(2,1)}, u32[]{:S(2)}) %copy-start) | copy-done | bytes 524312
  1.7 0.0 copy-start.1
  1.7 0.8 %copy-done.1 = bf16[32,512]{1,0:T(8,128)(2,1)S(1)} copy-done((bf16[32,512]{1,0:T(8,128)(2,1)S(1)}, bf16[32,512]{1,0:T(8,128)(2,1)}, u32[]{:S(2)}) %copy-start.1) | copy-done | bytes 32792
  2.5 0.0 copy-start.2
  2.5 0.8 %copy-done.2 = bf16[32,512]{1,0:T(8,128)(2,1)S(1)} copy-done((bf16[32,512]{1,0:T(8,128)(2,1)S(1)}, bf16[32,512]{1,0:T(8,128)(2,1)}, u32[]{:S(2)}) %copy-start.2) | copy-done | bytes 32792
  3.2 67.0 %shard_map.55 = bf16[16,32,512]{2,1,0:T(8,128)(2,1)S(1)} custom-call(bf16[16,32,512]{2,1,0:T(8,128)(2,1)S(1)} %copy-done, bf16[32,512]{1,0:T(8,128)(2,1)S(1)} %copy-done.1, bf16[32,512]{1,0:T(8,128)(2,1)S(1)} %copy-done.2, s32[1,1,256]{2,1,0:T(1,128)S(1)} %copy-done.3, s32[1,1]{1,0:T(1,128)S(6)} %copy.7.count), custom_call_target="tpu_custom_call" | custom-call | tf_op jit(solution)/shard_map/pallas_call | solution.py:445
  70.2 0.8 %copy.8 = bf16[16,32,512]{2,1,0:T(8,128)(2,1)} copy(bf16[16,32,512]{2,1,0:T(8,128)(2,1)S(1)} %shard_map.55) | data formatting | bytes 1048576
Async XLA Ops:
  0.0 0.7 copy-start.3
  0.7 1.0 %copy-start = (bf16[16,32,512]{2,1,0:T(8,128)(2,1)S(1)}, bf16[16,32,512]{2,1,0:T(8,128)(2,1)}, u32[]{:S(2)}) copy-start(bf16[16,32,512]{2,1,0:T(8,128)(2,1)} %ens.1) | copy-start | bytes 1572868
  1.7 0.8 %copy-start.1 = (bf16[32,512]{1,0:T(8,128)(2,1)S(1)}, bf16[32,512]{1,0:T(8,128)(2,1)}, u32[]{:S(2)}) copy-start(bf16[32,512]{1,0:T(8,128)(2,1)} %value.1) | copy-start | bytes 98308
  2.5 0.8 %copy-start.2 = (bf16[32,512]{1,0:T(8,128)(2,1)S(1)}, bf16[32,512]{1,0:T(8,128)(2,1)}, u32[]{:S(2)}) copy-start(bf16[32,512]{1,0:T(8,128)(2,1)} %precision.1) | copy-start | bytes 98308

commit v2 on v1

v2 whole, which is shorter than its diff:
```python
import functools
import math

import jax
import jax.numpy as jnp
from jax import lax
from jax.experimental import pallas as pl
from jax.experimental.pallas import tpu as pltpu
from jax.sharding import PartitionSpec as P

TILE = 32
ITERS = 5
LANES = 128
MESH = pl.DeviceIdType.MESH
F32 = jnp.float32
BF16 = jnp.bfloat16


def swap_blocks(parts):
    lane = lax.broadcasted_iota(jnp.int32, parts[0].shape, 1)
    low = lane < 64
    even = (lane // 32) % 2 == 0
    half = []
    for a, b in ((parts[0], parts[2]), (parts[1], parts[3])):
        half.append(
            (
                jnp.where(low, a, pltpu.roll(b, 64, 1)),
                jnp.where(low, pltpu.roll(a, 64, 1), b),
            )
        )
    result = []
    for which in range(2):
        a, b = half[0][which], half[1][which]
        result.append(jnp.where(even, a, pltpu.roll(b, 32, 1)))
        result.append(jnp.where(even, pltpu.roll(a, 96, 1), b))
    return result


def split(a):
    high = a.astype(BF16)
    return high, (a - high.astype(F32)).astype(BF16)


def product(a, b):
    return (
        jnp.dot(a[0], b[0], preferred_element_type=F32)
        + jnp.dot(a[0], b[1], preferred_element_type=F32)
        + jnp.dot(a[1], b[0], preferred_element_type=F32)
    )


def window_base(tile):
    return jnp.clip((tile * TILE + LANES - TILE // 2) // LANES - 1, 0, 2)


def padded_base(tile):
    return (tile * TILE + LANES - TILE // 2) // LANES


def column_select(cells, tile, first):
    column = cells % (2 * TILE) + (tile * TILE - TILE // 2 - first)
    place = lax.broadcasted_iota(jnp.int32, (2 * LANES, cells.shape[1]), 0)
    return jnp.where(place == column, F32(1.0), F32(0.0)).astype(BF16)


def fold_rows(parts):
    place = lax.broadcasted_iota(jnp.int32, parts[0].shape, 0)
    distance = 1
    while len(parts) > 1:
        odd = (place // distance) % 2 == 1
        parts = [
            jnp.where(odd, b, a) + pltpu.roll(jnp.where(odd, a, b), distance, 0)
            for a, b in zip(parts[::2], parts[1::2])
        ]
        distance *= 2
    return parts[0]


def row_select(columns, rows, members):
    slots = columns.shape[1]
    place = lax.broadcasted_iota(jnp.int32, (8, slots), 0)
    masks = [place + 8 * q == rows for q in range(4)]
    chosen = []
    for m in range(members):
        part = jnp.zeros((8, slots), F32)
        for q in range(4):
            at = m * TILE + 8 * q
            part = jnp.where(masks[q], columns[at : at + 8], part)
        chosen.append(part)
    return jnp.concatenate([fold_rows(chosen[m : m + 8]) for m in range(0, members, 8)], axis=0)


def own_rows(cells):
    return cells // (2 * TILE) - TILE // 2


def halo_rows(cells, first, last):
    row = cells // (2 * TILE)
    above = jnp.where(first, -1, row)
    below = jnp.where(last, -1, row - TILE)
    return jnp.where(row < TILE // 2, above, jnp.where(row >= 3 * TILE // 2, below, -1))


def kernel(
    regions,
    bands,
    ens,
    value,
    precision,
    index,
    count,
    out,
    held,
    halo,
    planes,
    planes_halo,
    cells_all,
    live_count,
    shuffle,
    main_send,
    main_recv,
    selected,
    obs_send,
    obs_recv,
    back_send,
    back_recv,
    load_sems,
    halo_sems,
    plane_sems,
    cell_sems,
    main_sems,
    obs_sems,
    back_sems,
):
    r = lax.axis_index("region")
    g = lax.axis_index("grp")
    up = lax.rem(g + bands - 1, bands)
    down = lax.rem(g + 1, bands)
    members = ens.shape[0]
    total = members * regions
    half = TILE // 2
    slots = index.shape[2]
    columns_all = ens.shape[2]
    groups = regions // 4
    chips = regions // 2
    first_group = r // 4
    chip, core = r // 2, lax.rem(r, 2)

    def peer(d):
        return lax.rem(r + d, regions)

    def ring_order(distances):
        return [
            2 * lax.rem(chip + d % chips, chips) + (1 - core if other else core)
            for d in distances
            for other in (0, 1)
            if d % chips or other
        ]

    barrier = pltpu.get_barrier_semaphore()
    for to in ring_order((4, 3, -3, 2, -2, 1, -1, 0)):
        pl.semaphore_signal(barrier, inc=1, device_id={"region": to}, device_id_type=MESH)
    for band in (up, down):
        pl.semaphore_signal(barrier, inc=1, device_id={"grp": band}, device_id_type=MESH)
    base_lanes = pl.ds(pl.multiple_of(window_base(r) * LANES, LANES), 2 * LANES)
    loads = [
        pltpu.make_async_copy(src, dst, load_sems.at[n])
        for n, (src, dst) in enumerate(
            (
                (ens, held.at[:, :, LANES : LANES + columns_all]),
                (value.at[:, base_lanes], planes.at[0]),
                (precision.at[:, base_lanes], planes.at[1]),
                (index.at[0], cells_all.at[r]),
                (count, live_count),
            )
        )
    ]
    for copy in loads:
        copy.start()
    zeros = jnp.zeros((members, TILE, LANES), BF16)
    for side in (slice(0, LANES), slice(LANES + columns_all, 2 * LANES + columns_all)):
        held[:, :, side] = zeros
        halo[:, :, side] = zeros
    loads[0].wait()

    def group_lanes(group):
        return pl.ds(pl.multiple_of(group * LANES, LANES), LANES)

    def padded_lanes(group):
        return group_lanes(group + 1)

    def pack_group(group, carry):
        lanes = padded_lanes(group)
        for m in range(members):
            block = held[m, :, lanes].astype(F32)
            parts = swap_blocks([block[8 * q : 8 * q + 8] for q in range(4)])
            for t in range(4):
                shuffle[t, m * 8 : m * 8 + 8, :] = parts[t]
        for t in range(4):
            for s in range(8):
                main_send[4 * group + t, :, s * LANES : (s + 1) * LANES] = shuffle[
                    t, pl.ds(s, members, stride=8), :
                ].astype(BF16)
        return carry

    lax.fori_loop(0, groups, pack_group, 0)
    for copy in loads[1:]:
        copy.wait()
    main_recv[r] = main_send[r]
    pl.semaphore_wait(barrier, regions + 1)

    def band_copy(src, dst, sems, at, side):
        return pltpu.make_async_remote_copy(
            src_ref=src,
            dst_ref=dst,
            send_sem=sems.at[0, at],
            recv_sem=sems.at[1, at],
            device_id={"grp": (down, up)[side]},
            device_id_type=MESH,
        )

    rows_out = (pl.ds(half, half), pl.ds(0, half))
    rows_in = (pl.ds(0, half), pl.ds(half, half))

    def halo_copies(step):
        group = lax.rem(first_group + step, groups)
        lanes = padded_lanes(group)
        return [
            band_copy(
                held.at[:, rows_out[side], lanes],
                halo.at[:, rows_in[side], lanes],
                halo_sems,
                2 * group + side,
                side,
            )
            for side in range(2)
        ]

    plane_copies = [
        band_copy(
            planes.at[n, rows_out[side], :],
            planes_halo.at[n, rows_in[side], :],
            plane_sems,
            2 * n + side,
            side,
        )
        for n in range(2)
        for side in range(2)
    ]

    def cell_copy(to, slot):
        return pltpu.make_async_remote_copy(
            src_ref=cells_all.at[r],
            dst_ref=cells_all.at[slot],
            send_sem=cell_sems.at[0, to],
            recv_sem=cell_sems.at[1, slot],
            device_id={"region": to},
            device_id_type=MESH,
        )

    def block_copy(send, recv, sems, to, slot):
        return pltpu.make_async_remote_copy(
            src_ref=send.at[to],
            dst_ref=recv.at[slot],
            send_sem=sems.at[0, to],
            recv_sem=sems.at[1, slot],
            device_id={"region": to},
            device_id_type=MESH,
        )

    def send_main(distances):
        for to in ring_order(distances):
            block_copy(main_send, main_recv, main_sems, to, r).start()

    for to in ring_order((4, 3, -3, 2, -2, 1, -1, 0)):
        cell_copy(to, r).start()
    for step in range(groups):
        for copy in halo_copies(step):
            copy.start()
    for copy in plane_copies:
        copy.start()
    send_main((3, -3, 1, -1))

    def choose(source, rows, tile):
        base = padded_base(tile)
        lanes = pl.ds(pl.multiple_of(base * LANES, LANES), 2 * LANES)
        columns = jnp.dot(
            source[:, :, lanes].reshape(members * TILE, 2 * LANES),
            column_select(cells_all[tile], tile, (base - 1) * LANES),
            preferred_element_type=F32,
        )
        return row_select(columns, rows, members)

    def tiles_of(step):
        return [peer_tile(4 * step + n) for n in range(4)]

    def peer_tile(n):
        return lax.rem(4 * first_group + 1 + n, regions)

    def from_own(step, carry):
        tiles = tiles_of(step)
        for tile in tiles:

            @pl.when(tile != r)
            def _():
                cell_copy(tile, tile).wait_recv()

        for tile in tiles:
            selected[tile] = choose(held, own_rows(cells_all[tile]), tile)
        return carry

    lax.fori_loop(0, groups, from_own, 0)

    def from_halo(step, carry):
        @pl.when(step == 0)
        def _():
            for copy in halo_copies(0):
                copy.wait_recv()

        @pl.when(step < groups - 1)
        def _():
            for copy in halo_copies(step + 1):
                copy.wait_recv()

        tiles = tiles_of(step)
        for tile in tiles:
            rows = halo_rows(cells_all[tile], g == 0, g == bands - 1)
            obs_send[tile] = (selected[tile] + choose(halo, rows, tile)).astype(BF16)
        for tile in tiles:

            @pl.when(tile != r)
            def _():
                block_copy(obs_send, obs_recv, obs_sems, tile, r).start()

        return carry

    lax.fori_loop(0, groups, from_halo, 0)
    send_main((4, 2, -2, 0))
    obs_recv[r] = obs_send[r]

    for copy in plane_copies:
        copy.wait_recv()
    cells = cells_all[r]
    fields = jnp.concatenate([planes[0], planes_halo[0], planes[1], planes_halo[1]], axis=0)
    columns = jnp.dot(fields, column_select(cells, r, window_base(r) * LANES), preferred_element_type=F32)
    place = lax.broadcasted_iota(jnp.int32, (TILE, slots), 0)
    at_own = place == own_rows(cells)
    at_halo = place == halo_rows(cells, g == 0, g == bands - 1)

    def field(n):
        own = jnp.where(at_own, columns[2 * n * TILE : (2 * n + 1) * TILE], F32(0.0))
        beside = jnp.where(at_halo, columns[(2 * n + 1) * TILE : (2 * n + 2) * TILE], F32(0.0))
        return jnp.sum(own + beside, axis=0, keepdims=True)

    values_at = field(0)
    precision_at = field(1)
    offset_y = (cells // (2 * TILE)).astype(F32) - (TILE - 0.5)
    offset_x = (cells % (2 * TILE)).astype(F32) - (TILE - 0.5)
    length = 0.375 * TILE
    inflation = jnp.exp(-(offset_y * offset_y + offset_x * offset_x) / (2.0 * length * length))
    live = lax.broadcasted_iota(jnp.int32, (1, slots), 1) < live_count[...]
    weight = jnp.where(live, precision_at * inflation, F32(0.0))

    def wait_block(recv, sems):
        def body(d, carry):
            src = peer(d)
            block_copy(recv, recv, sems, src, src).wait_recv()
            return carry

        lax.fori_loop(1, regions, body, 0)

    wait_block(obs_recv, obs_sems)

    raw = obs_recv[...].reshape(total, slots).astype(F32)
    average = jnp.sum(raw, axis=0, keepdims=True) * (1.0 / total)
    pert = (raw - average).astype(BF16)
    scaled = weight * (values_at - average)
    weighted = (pert.astype(F32) * weight).astype(BF16)
    across = (((1,), (1,)), ((), ()))
    diagonal = lax.broadcasted_iota(jnp.int32, (total, total), 0) == lax.broadcasted_iota(
        jnp.int32, (total, total), 1
    )

    def plus_identity(scale, a):
        return a + jnp.where(diagonal, F32(scale), F32(0.0))

    system = plus_identity(
        total - 1.0, lax.dot_general(pert, weighted, across, preferred_element_type=F32)
    )
    squares = jnp.sum(system * system, axis=0, keepdims=True)
    frobenius = jnp.sqrt(jnp.sum(squares, axis=1, keepdims=True))
    inverse_frobenius = 1.0 / frobenius

    scaled_high = scaled.astype(BF16)
    rest = scaled - scaled_high.astype(F32)
    scaled_mid = rest.astype(BF16)
    scaled_low = (rest - scaled_mid.astype(F32)).astype(BF16)

    def stack(*rows):
        n = rows[0].shape[1]
        place = lax.broadcasted_iota(jnp.int32, (16, n), 0)
        whole = jnp.zeros((16, n), F32)
        for at, row in enumerate(rows):
            whole = jnp.where(place == at, row.astype(F32), whole)
        return whole.astype(BF16)

    projected = jnp.sum(
        lax.dot_general(
            stack(scaled_high, scaled_mid, scaled_low), pert, across, preferred_element_type=F32
        ),
        axis=0,
        keepdims=True,
    )

    start = system * inverse_frobenius
    root = split(start)
    inverse_root = plus_identity(1.5, -0.5 * start)
    factor = split(inverse_root)
    inverse_pair = factor
    root = split(product(root, factor))
    for number in range(1, ITERS):
        factor = split(plus_identity(1.5, -0.5 * product(root, inverse_pair)))
        if number < ITERS - 1:
            root = split(product(factor, root))
        inverse_root = product(inverse_pair, factor)
        inverse_pair = split(inverse_root)

    def row_product(row):
        pair = stack(*split(row))
        first = jnp.dot(pair, inverse_pair[0], preferred_element_type=F32)
        second = jnp.dot(pair, inverse_pair[1], preferred_element_type=F32)
        return first[0:1] + first[1:2] + second[0:1]

    mean_weight = row_product(row_product(projected)) * inverse_frobenius
    spread = math.sqrt(total - 1.0) / jnp.sqrt(frobenius)
    weights = (spread * inverse_root + mean_weight).astype(BF16)

    wait_block(main_recv, main_sems)
    cell_total = main_recv.shape[2]
    step = 2 * LANES
    for n in range(cell_total // step):
        at = slice(n * step, (n + 1) * step)
        prior = main_recv[:, :, at].reshape(total, step).astype(F32)
        mean = jnp.sum(prior, axis=0, keepdims=True) * (1.0 / total)
        update = jnp.dot(weights, (prior - mean).astype(BF16), preferred_element_type=F32)
        back_send[:, :, at] = (update + mean).astype(BF16).reshape(regions, members, step)

    for to in ring_order((4, 3, -3, 2, -2, 1, -1, 0)):
        block_copy(back_send, back_recv, back_sems, to, r).start()
    back_recv[r] = back_send[r]

    def unpack_group(step, carry):
        group = lax.rem(first_group + 2 + step, groups)
        lanes = group_lanes(group)
        for t in range(4):
            tile = 4 * group + t

            @pl.when(tile != r)
            def _():
                block_copy(back_recv, back_recv, back_sems, tile, tile).wait_recv()

        for t in range(4):
            for s in range(8):
                shuffle[t, pl.ds(s, members, stride=8), :] = back_recv[
                    4 * group + t, :, s * LANES : (s + 1) * LANES
                ].astype(F32)
        for m in range(members):
            parts = swap_blocks([shuffle[t, m * 8 : m * 8 + 8, :] for t in range(4)])
            out[m, :, lanes] = jnp.concatenate(parts, axis=0).astype(BF16)
        return carry

    lax.fori_loop(0, groups, unpack_group, 0)

    def finish_sends(d, carry):
        to = peer(d)
        cell_copy(to, r).wait_send()
        block_copy(main_send, main_recv, main_sems, to, r).wait_send()
        block_copy(obs_send, obs_recv, obs_sems, to, r).wait_send()
        block_copy(back_send, back_recv, back_sems, to, r).wait_send()
        return carry

    lax.fori_loop(1, regions, finish_sends, 0)
    for step in range(groups):
        for copy in halo_copies(step):
            copy.wait_send()
    for copy in plane_copies:
        copy.wait_send()


def solution(mesh):
    regions = mesh.shape["region"]
    bands = mesh.shape["grp"]

    def shards(ensemble, obs_value, obs_prec, obs_index, obs_count):
        members, rows, columns = ensemble.shape
        slots = obs_index.shape[2]
        cells = rows * TILE
        return pl.pallas_call(
            functools.partial(kernel, regions, bands),
            out_shape=jax.ShapeDtypeStruct(ensemble.shape, BF16),
            in_specs=[pl.BlockSpec(memory_space=pl.ANY)] * 5,
            out_specs=pl.BlockSpec(memory_space=pltpu.VMEM),
            scratch_shapes=[
                pltpu.VMEM((members, rows, columns + 2 * LANES), BF16),
                pltpu.VMEM((members, rows, columns + 2 * LANES), BF16),
                pltpu.VMEM((2, rows, 2 * LANES), BF16),
                pltpu.VMEM((2, rows, 2 * LANES), BF16),
                pltpu.VMEM((regions, 1, slots), jnp.int32),
                pltpu.VMEM((1, 1), jnp.int32),
                pltpu.VMEM((4, members * 8, LANES), F32),
                pltpu.VMEM((regions, members, cells), BF16),
                pltpu.VMEM((regions, members, cells), BF16),
                pltpu.VMEM((regions, members, slots), F32),
                pltpu.VMEM((regions, members, slots), BF16),
                pltpu.VMEM((regions, members, slots), BF16),
                pltpu.VMEM((regions, members, cells), BF16),
                pltpu.VMEM((regions, members, cells), BF16),
                pltpu.SemaphoreType.DMA((5,)),
                pltpu.SemaphoreType.DMA((2, regions // 2)),
                pltpu.SemaphoreType.DMA((2, 4)),
                pltpu.SemaphoreType.DMA((2, regions)),
                pltpu.SemaphoreType.DMA((2, regions)),
                pltpu.SemaphoreType.DMA((2, regions)),
                pltpu.SemaphoreType.DMA((2, regions)),
            ],
            compiler_params=pltpu.CompilerParams(
                collective_id=0, has_side_effects=True, vmem_limit_bytes=60 * 1024 * 1024
            ),
        )(ensemble, obs_value, obs_prec, obs_index, obs_count)

    placed = (
        P("region", "grp", None),
        P("grp", None),
        P("grp", None),
        P("grp", "region", None),
        P("grp", "region"),
    )
    return jax.shard_map(
        shards, mesh=mesh, in_specs=placed, out_specs=P("region", "grp", None), check_vma=False
    )
```

time: 71.4 us -> 55.3 us (0.77)
  Pallas kernels: 67 us -> 52.6 us
  local copies, waits for them, and re-layouts: 3.36 us -> 1.88 us
    pallas_call x1, Pallas kernels: 67 us -> 52.6 us  [shards(): pl.pallas_call(functools.partial(kernel, regions, bands), out_shape=jax.S...]
    unnamed x9 -> x1, local copies, waits for them, and re-layouts: 3.36 us -> 1.88 us
where the time goes in v2:
time: 55.3 us; the launch traced here: 55.2 us
  Pallas kernels  52.6 us (95%)
  local copies, waits for them, and re-layouts  1.88 us (3%)
  between operations  0.66 us (1%)
    pallas_call x1, Pallas kernels, shards(): pl.pallas_call(functools.partial(kernel, regions, bands), out_shape=jax.S...  52.6 us
    unnamed x1, local copies, waits for them, and re-layouts  1.88 us

profile of v2, /device:TPU:1, one launch (start us, length us, event | category | flops | bytes accessed | tf_op | source)
XLA Modules:
  0.0 55.2 jit_solution(12997599750257144958)
XLA Ops:
  0.7 52.6 %shard_map.55 = bf16[16,32,512]{2,1,0:T(8,128)(2,1)} custom-call(bf16[16,32,512]{2,1,0:T(8,128)(2,1)} %ens.1, bf16[32,512]{1,0:T(8,128)(2,1)} %value.1, bf16[32,512]{1,0:T(8,128)(2,1)} %precision.1, s32[1,1,256]{2,1,0:T(1,128)} %index.1, s32[1,1]{1,0:T(1,128)S(6)} %copy.7.count), custom_call_target="tpu_custom_call" | custom-call | tf_op jit(solution)/shard_map/pallas_call | solution.py:498
  53.3 1.9 %copy.8 = bf16[16,32,512]{2,1,0:T(8,128)(2,1)} copy(bf16[16,32,512]{2,1,0:T(8,128)(2,1)} %shard_map.55) | data formatting | bytes 1048576

commit v3 on v2

--- a/solution.py
+++ b/solution.py
@@ -160,8 +160,16 @@
     barrier = pltpu.get_barrier_semaphore()
     for to in ring_order((4, 3, -3, 2, -2, 1, -1, 0)):
         pl.semaphore_signal(barrier, inc=1, device_id={"region": to}, device_id_type=MESH)
-    for band in (up, down):
-        pl.semaphore_signal(barrier, inc=1, device_id={"grp": band}, device_id_type=MESH)
+    has_side = (g < bands - 1, g > 0)
+    band_peers = (down, up)
+    for side in range(2):
+
+        @pl.when(has_side[side])
+        def _():
+            pl.semaphore_signal(
+                barrier, inc=1, device_id={"grp": band_peers[side]}, device_id_type=MESH
+            )
+
     base_lanes = pl.ds(pl.multiple_of(window_base(r) * LANES, LANES), 2 * LANES)
     loads = [
         pltpu.make_async_copy(src, dst, load_sems.at[n])
@@ -181,6 +189,17 @@
     for side in (slice(0, LANES), slice(LANES + columns_all, 2 * LANES + columns_all)):
         held[:, :, side] = zeros
         halo[:, :, side] = zeros
+    for side in range(2):
+
+        @pl.when(jnp.logical_not(has_side[1 - side]))
+        def _():
+            halo[:, side * half : (side + 1) * half, :] = jnp.zeros(
+                (members, half, columns_all + 2 * LANES), BF16
+            )
+            planes_halo[:, side * half : (side + 1) * half, :] = jnp.zeros(
+                (2, half, 2 * LANES), BF16
+            )
+
     loads[0].wait()
 
     def group_lanes(group):
@@ -207,7 +226,8 @@
     for copy in loads[1:]:
         copy.wait()
     main_recv[r] = main_send[r]
-    pl.semaphore_wait(barrier, regions + 1)
+    bands_beside = jnp.where(g > 0, 1, 0) + jnp.where(g < bands - 1, 1, 0)
+    pl.semaphore_wait(barrier, regions - 1 + bands_beside)
 
     def band_copy(src, dst, sems, at, side):
         return pltpu.make_async_remote_copy(
@@ -215,38 +235,67 @@
             dst_ref=dst,
             send_sem=sems.at[0, at],
             recv_sem=sems.at[1, at],
-            device_id={"grp": (down, up)[side]},
+            device_id={"grp": band_peers[side]},
             device_id_type=MESH,
         )
 
     rows_out = (pl.ds(half, half), pl.ds(0, half))
     rows_in = (pl.ds(0, half), pl.ds(half, half))
 
-    def halo_copies(step):
+    def halo_copy(step, side):
         group = lax.rem(first_group + step, groups)
         lanes = padded_lanes(group)
-        return [
-            band_copy(
-                held.at[:, rows_out[side], lanes],
-                halo.at[:, rows_in[side], lanes],
-                halo_sems,
-                2 * group + side,
-                side,
-            )
-            for side in range(2)
-        ]
-
-    plane_copies = [
-        band_copy(
+        return band_copy(
+            held.at[:, rows_out[side], lanes],
+            halo.at[:, rows_in[side], lanes],
+            halo_sems,
+            2 * group + side,
+            side,
+        )
+
+    def plane_copy(n, side):
+        return band_copy(
             planes.at[n, rows_out[side], :],
             planes_halo.at[n, rows_in[side], :],
             plane_sems,
             2 * n + side,
             side,
         )
-        for n in range(2)
-        for side in range(2)
-    ]
+
+    def start_halo():
+        for side in range(2):
+
+            @pl.when(has_side[side])
+            def _():
+                for step in range(groups):
+                    halo_copy(step, side).start()
+                for n in range(2):
+                    plane_copy(n, side).start()
+
+    def receive_halo(step):
+        for side in range(2):
+
+            @pl.when(has_side[1 - side])
+            def _():
+                halo_copy(step, side).wait_recv()
+
+    def receive_planes():
+        for side in range(2):
+
+            @pl.when(has_side[1 - side])
+            def _():
+                for n in range(2):
+                    plane_copy(n, side).wait_recv()
+
+    def finish_halo():
+        for side in range(2):
+
+            @pl.when(has_side[side])
+            def _():
+                for step in range(groups):
+                    halo_copy(step, side).wait_send()
+                for n in range(2):
+                    plane_copy(n, side).wait_send()
 
     def cell_copy(to, slot):
         return pltpu.make_async_remote_copy(
@@ -274,12 +323,8 @@
 
     for to in ring_order((4, 3, -3, 2, -2, 1, -1, 0)):
         cell_copy(to, r).start()
-    for step in range(groups):
-        for copy in halo_copies(step):
-            copy.start()
-    for copy in plane_copies:
-        copy.start()
-    send_main((3, -3, 1, -1))
+    start_halo()
+    send_main((4, 3, -3, 1, -1))
 
     def choose(source, rows, tile):
         base = padded_base(tile)
@@ -314,13 +359,11 @@
     def from_halo(step, carry):
         @pl.when(step == 0)
         def _():
-            for copy in halo_copies(0):
-                copy.wait_recv()
+            receive_halo(0)
 
         @pl.when(step < groups - 1)
         def _():
-            for copy in halo_copies(step + 1):
-                copy.wait_recv()
+            receive_halo(step + 1)
 
         tiles = tiles_of(step)
         for tile in tiles:
@@ -335,11 +378,10 @@
         return carry
 
     lax.fori_loop(0, groups, from_halo, 0)
-    send_main((4, 2, -2, 0))
+    send_main((2, -2, 0))
     obs_recv[r] = obs_send[r]
 
-    for copy in plane_copies:
-        copy.wait_recv()
+    receive_planes()
     cells = cells_all[r]
     fields = jnp.concatenate([planes[0], planes_halo[0], planes[1], planes_halo[1]], axis=0)
     columns = jnp.dot(fields, column_select(cells, r, window_base(r) * LANES), preferred_element_type=F32)
@@ -480,11 +522,7 @@
         return carry
 
     lax.fori_loop(1, regions, finish_sends, 0)
-    for step in range(groups):
-        for copy in halo_copies(step):
-            copy.wait_send()
-    for copy in plane_copies:
-        copy.wait_send()
+    finish_halo()
 
 
 def solution(mesh):
@@ -497,7 +535,7 @@
         cells = rows * TILE
         return pl.pallas_call(
             functools.partial(kernel, regions, bands),
-            out_shape=jax.ShapeDtypeStruct(ensemble.shape, BF16),
+            out_shape=pltpu.VMEM(ensemble.shape, BF16),
             in_specs=[pl.BlockSpec(memory_space=pl.ANY)] * 5,
             out_specs=pl.BlockSpec(memory_space=pltpu.VMEM),
             scratch_shapes=[

time: 55.3 us -> 49.2 us (0.89); the launches traced: 55.2 us -> 48.3 us
  Pallas kernels: 52.6 us -> 46.9 us
  local copies, waits for them, and re-layouts: 1.88 us -> 0.8 us
    pallas_call x1, Pallas kernels: 52.6 us -> 46.9 us  [shards(): pl.pallas_call(functools.partial(kernel, regions, bands), out_shape=pltpu...]
    unnamed x1, local copies, waits for them, and re-layouts: 1.88 us -> 0.8 us
where the time goes in v3:
time: 49.2 us; the launch traced here: 48.3 us
  Pallas kernels  46.9 us (95%)
  local copies, waits for them, and re-layouts  0.8 us (2%)
  between operations  0.66 us (1%)
    pallas_call x1, Pallas kernels, shards(): pl.pallas_call(functools.partial(kernel, regions, bands), out_shape=pltpu...  46.9 us

profile of v3, /device:TPU:1, one launch (start us, length us, event | category | flops | bytes accessed | tf_op | source)
XLA Modules:
  0.0 48.3 jit_solution(3462066573120246563)
XLA Ops:
  0.7 46.9 %shard_map.55 = bf16[16,32,512]{2,1,0:T(8,128)(2,1)S(1)} custom-call(bf16[16,32,512]{2,1,0:T(8,128)(2,1)} %ens.1, bf16[32,512]{1,0:T(8,128)(2,1)} %value.1, bf16[32,512]{1,0:T(8,128)(2,1)} %precision.1, s32[1,1,256]{2,1,0:T(1,128)} %index.1, s32[1,1]{1,0:T(1,128)S(6)} %copy.8.count), custom_call_target="tpu_custom_call" | custom-call | tf_op jit(solution)/shard_map/pallas_call | solution.py:536
  47.5 0.8 %copy.7 = bf16[16,32,512]{2,1,0:T(8,128)(2,1)} copy(bf16[16,32,512]{2,1,0:T(8,128)(2,1)S(1)} %shard_map.55) | data formatting | bytes 1048576

commit v4 on v3

--- a/solution.py
+++ b/solution.py
@@ -11,6 +11,7 @@
 TILE = 32
 ITERS = 5
 LANES = 128
+START = 1
 MESH = pl.DeviceIdType.MESH
 F32 = jnp.float32
 BF16 = jnp.bfloat16
@@ -57,9 +58,9 @@
     return (tile * TILE + LANES - TILE // 2) // LANES
 
 
-def column_select(cells, tile, first):
+def column_select(cells, tile, first, width):
     column = cells % (2 * TILE) + (tile * TILE - TILE // 2 - first)
-    place = lax.broadcasted_iota(jnp.int32, (2 * LANES, cells.shape[1]), 0)
+    place = lax.broadcasted_iota(jnp.int32, (width, cells.shape[1]), 0)
     return jnp.where(place == column, F32(1.0), F32(0.0)).astype(BF16)
 
 
@@ -243,7 +244,7 @@
     rows_in = (pl.ds(0, half), pl.ds(half, half))
 
     def halo_copy(step, side):
-        group = lax.rem(first_group + step, groups)
+        group = lax.rem(first_group + START + step, groups)
         lanes = padded_lanes(group)
         return band_copy(
             held.at[:, rows_out[side], lanes],
@@ -321,70 +322,58 @@
         for to in ring_order(distances):
             block_copy(main_send, main_recv, main_sems, to, r).start()
 
+    start_halo()
     for to in ring_order((4, 3, -3, 2, -2, 1, -1, 0)):
         cell_copy(to, r).start()
-    start_halo()
-    send_main((4, 3, -3, 1, -1))
-
-    def choose(source, rows, tile):
-        base = padded_base(tile)
-        lanes = pl.ds(pl.multiple_of(base * LANES, LANES), 2 * LANES)
+    send_main((3, -3, 2, -2))
+
+    def choose(source, rows, tile, kind):
+        one_block = kind in (1, 2)
+        base = tile // 4 + 1 if one_block else padded_base(tile)
+        width = LANES if one_block else 2 * LANES
+        lanes = pl.ds(pl.multiple_of(base * LANES, LANES), width)
         columns = jnp.dot(
-            source[:, :, lanes].reshape(members * TILE, 2 * LANES),
-            column_select(cells_all[tile], tile, (base - 1) * LANES),
+            source[:, :, lanes].reshape(members * TILE, width),
+            column_select(cells_all[tile], tile, (base - 1) * LANES, width),
             preferred_element_type=F32,
         )
         return row_select(columns, rows, members)
 
-    def tiles_of(step):
-        return [peer_tile(4 * step + n) for n in range(4)]
-
-    def peer_tile(n):
-        return lax.rem(4 * first_group + 1 + n, regions)
-
     def from_own(step, carry):
-        tiles = tiles_of(step)
-        for tile in tiles:
+        group = lax.rem(first_group + jnp.where(step < 2, step, 5 - step), groups)
+        for kind in range(4):
+            tile = 4 * group + kind
 
             @pl.when(tile != r)
             def _():
                 cell_copy(tile, tile).wait_recv()
 
-        for tile in tiles:
-            selected[tile] = choose(held, own_rows(cells_all[tile]), tile)
+        for kind in range(4):
+            tile = 4 * group + kind
+            selected[tile] = choose(held, own_rows(cells_all[tile]), tile, kind)
         return carry
 
     lax.fori_loop(0, groups, from_own, 0)
 
-    def from_halo(step, carry):
-        @pl.when(step == 0)
-        def _():
-            receive_halo(0)
-
-        @pl.when(step < groups - 1)
-        def _():
-            receive_halo(step + 1)
-
-        tiles = tiles_of(step)
-        for tile in tiles:
+    for step, places in enumerate((range(2), range(2, 6), range(6, 10), range(10, 16))):
+        receive_halo(step)
+        tiles = [(lax.rem(4 * (first_group + START) + 1 + n, regions), (1 + n) % 4) for n in places]
+        for tile, kind in tiles:
             rows = halo_rows(cells_all[tile], g == 0, g == bands - 1)
-            obs_send[tile] = (selected[tile] + choose(halo, rows, tile)).astype(BF16)
-        for tile in tiles:
+            obs_send[tile] = (selected[tile] + choose(halo, rows, tile, kind)).astype(BF16)
+        for tile, _ in tiles:
 
             @pl.when(tile != r)
             def _():
                 block_copy(obs_send, obs_recv, obs_sems, tile, r).start()
 
-        return carry
-
-    lax.fori_loop(0, groups, from_halo, 0)
-    send_main((2, -2, 0))
+    send_main((4, 1, -1, 0))
     obs_recv[r] = obs_send[r]
 
     receive_planes()
     cells = cells_all[r]
     fields = jnp.concatenate([planes[0], planes_halo[0], planes[1], planes_halo[1]], axis=0)
-    columns = jnp.dot(fields, column_select(cells, r, window_base(r) * LANES), preferred_element_type=F32)
+    columns = jnp.dot(fields, column_select(cells, r, window_base(r) * LANES, 2 * LANES), preferred_element_type=F32)
     place = lax.broadcasted_iota(jnp.int32, (TILE, slots), 0)
     at_own = place == own_rows(cells)
     at_halo = place == halo_rows(cells, g == 0, g == bands - 1)
@@ -487,12 +476,12 @@
         update = jnp.dot(weights, (prior - mean).astype(BF16), preferred_element_type=F32)
         back_send[:, :, at] = (update + mean).astype(BF16).reshape(regions, members, step)
 
-    for to in ring_order((4, 3, -3, 2, -2, 1, -1, 0)):
+    for to in ring_order((1, -1, 2, -2, 3, -3, 4, 0)):
         block_copy(back_send, back_recv, back_sems, to, r).start()
     back_recv[r] = back_send[r]
 
     def unpack_group(step, carry):
-        group = lax.rem(first_group + 2 + step, groups)
+        group = lax.rem(first_group + step, groups)
         lanes = group_lanes(group)
         for t in range(4):
             tile = 4 * group + t

time: 49.2 us -> 47.3 us (0.961)
  Pallas kernels: 46.9 us -> 45.2 us
    pallas_call x1, Pallas kernels: 46.9 us -> 45.2 us  [shards(): pl.pallas_call(functools.partial(kernel, regions, bands), out_shape=pltpu...]
where the time goes in v4:
time: 47.3 us; the launch traced here: 46.7 us
  Pallas kernels  45.2 us (96%)
  local copies, waits for them, and re-layouts  0.8 us (2%)
  between operations  0.66 us (1%)
    pallas_call x1, Pallas kernels, shards(): pl.pallas_call(functools.partial(kernel, regions, bands), out_shape=pltpu...  45.2 us

profile of v4, /device:TPU:1, one launch (start us, length us, event | category | flops | bytes accessed | tf_op | source)
XLA Modules:
  0.0 46.7 jit_solution(12341191334881125880)
XLA Ops:
  0.7 45.2 %shard_map.55 = bf16[16,32,512]{2,1,0:T(8,128)(2,1)S(1)} custom-call(bf16[16,32,512]{2,1,0:T(8,128)(2,1)} %ens.1, bf16[32,512]{1,0:T(8,128)(2,1)} %value.1, bf16[32,512]{1,0:T(8,128)(2,1)} %precision.1, s32[1,1,256]{2,1,0:T(1,128)} %index.1, s32[1,1]{1,0:T(1,128)S(6)} %copy.8.count), custom_call_target="tpu_custom_call" | custom-call | tf_op jit(solution)/shard_map/pallas_call | solution.py:525
  45.9 0.8 %copy.7 = bf16[16,32,512]{2,1,0:T(8,128)(2,1)} copy(bf16[16,32,512]{2,1,0:T(8,128)(2,1)S(1)} %shard_map.55) | data formatting | bytes 1048576

commit v5 on v4

--- a/solution.py
+++ b/solution.py
@@ -43,11 +43,16 @@
 
 
 def product(a, b):
-    return (
-        jnp.dot(a[0], b[0], preferred_element_type=F32)
-        + jnp.dot(a[0], b[1], preferred_element_type=F32)
-        + jnp.dot(a[1], b[0], preferred_element_type=F32)
-    )
+    height = a[0].shape[0] // 2
+    blocks = []
+    for n in range(2):
+        rows = slice(n * height, (n + 1) * height)
+        blocks.append(
+            jnp.dot(a[0][rows], b[0], preferred_element_type=F32)
+            + jnp.dot(a[0][rows], b[1], preferred_element_type=F32)
+            + jnp.dot(a[1][rows], b[0], preferred_element_type=F32)
+        )
+    return jnp.concatenate(blocks, axis=0)
 
 
 def window_base(tile):
@@ -480,6 +485,16 @@
         block_copy(back_send, back_recv, back_sems, to, r).start()
     back_recv[r] = back_send[r]
 
+    def finish_sends(d, carry):
+        to = peer(d)
+        cell_copy(to, r).wait_send()
+        block_copy(main_send, main_recv, main_sems, to, r).wait_send()
+        block_copy(obs_send, obs_recv, obs_sems, to, r).wait_send()
+        return carry
+
+    lax.fori_loop(1, regions, finish_sends, 0)
+    finish_halo()
+
     def unpack_group(step, carry):
         group = lax.rem(first_group + step, groups)
         lanes = group_lanes(group)
@@ -502,16 +517,11 @@
 
     lax.fori_loop(0, groups, unpack_group, 0)
 
-    def finish_sends(d, carry):
-        to = peer(d)
-        cell_copy(to, r).wait_send()
-        block_copy(main_send, main_recv, main_sems, to, r).wait_send()
-        block_copy(obs_send, obs_recv, obs_sems, to, r).wait_send()
-        block_copy(back_send, back_recv, back_sems, to, r).wait_send()
+    def finish_back(d, carry):
+        block_copy(back_send, back_recv, back_sems, peer(d), r).wait_send()
         return carry
 
-    lax.fori_loop(1, regions, finish_sends, 0)
-    finish_halo()
+    lax.fori_loop(1, regions, finish_back, 0)
 
 
 def solution(mesh):

time: 47.3 us -> 46.5 us (0.983); the launches traced: 46.7 us -> 46.4 us
  no operation moved by 1% of the time
where the time goes in v5:
time: 46.5 us; the launch traced here: 46.4 us
  Pallas kernels  44.9 us (97%)
  local copies, waits for them, and re-layouts  0.8 us (2%)
  between operations  0.66 us (1%)
    pallas_call x1, Pallas kernels, shards(): pl.pallas_call(functools.partial(kernel, regions, bands), out_shape=pltpu...  44.9 us

profile of v5, /device:TPU:1, one launch (start us, length us, event | category | flops | bytes accessed | tf_op | source)
XLA Modules:
  0.0 46.4 jit_solution(14471547692006808652)
XLA Ops:
  0.7 44.9 %shard_map.55 = bf16[16,32,512]{2,1,0:T(8,128)(2,1)S(1)} custom-call(bf16[16,32,512]{2,1,0:T(8,128)(2,1)} %ens.1, bf16[32,512]{1,0:T(8,128)(2,1)} %value.1, bf16[32,512]{1,0:T(8,128)(2,1)} %precision.1, s32[1,1,256]{2,1,0:T(1,128)} %index.1, s32[1,1]{1,0:T(1,128)S(6)} %copy.8.count), custom_call_target="tpu_custom_call" | custom-call | tf_op jit(solution)/shard_map/pallas_call | solution.py:535
  45.6 0.8 %copy.7 = bf16[16,32,512]{2,1,0:T(8,128)(2,1)} copy(bf16[16,32,512]{2,1,0:T(8,128)(2,1)S(1)} %shard_map.55) | data formatting | bytes 1048576
